TPU v7x, 128 devices: a whole 4x4x4 slice. The times are simulated.
128 devices in a mesh: row: 16 (over x, z), col: 8 (over y, core).
Axes of the slice: x: 4, y: 4, z: 4, core: 2. Of those that a mesh axis runs over, the one named last changes fastest.
Arguments:
- root_inverse: float32 [2, 2048, 4, 1024], P(None, 'row', None, 'col'), as said below
- child_coupling: float32 [2, 2, 2048, 2, 1024], P(None, None, 'row', None, 'col'), may hold values from -0.046875 to 0.046875
- child_inverse: float32 [2, 1, 2048, 2, 1024], P(None, None, 'row', None, 'col'), as said below
- pattern: int32 [2, 32], replicated, may hold values 0 or 1
Outputs:
- sigma_root: float32 [2, 2048, 4, 1024], P(None, 'row', None, 'col')
- sigma_coupling: float32 [2, 2, 2048, 2, 1024], P(None, None, 'row', None, 'col')
- sigma_child: float32 [2, 128, 2, 1024], P(None, None, None, 'col')
Inputs may be any that keep to these rules, and one draw needn't show every extreme that they name: `root_inverse`: read row-major as a 4096 x 4096 matrix it is lower triangular with a positive diagonal. `child_inverse`: read row-major each child's 2048 x 2048 matrix is lower triangular with a positive diagonal. `pattern`: 1 where child j's separator couples to root supernode i, else 0.
All inputs are finite; a program needn't handle non-finite values.
Results may differ from a plain program's by a relative error of at most 0.00013.
Values sent between devices are 32-bit elements; how exact they have to be, the bound alone decides.
No kernel may reach another device: no remote copies, remote signals or barrier semaphores. Data moves between devices by JAX's collectives and lax.ppermute only.
A program may use at most 128 MiB of HBM per device.

v0:
```python
import jax
import jax.numpy as jnp
from jax import lax
from jax.sharding import PartitionSpec as P

B = 128
NR = 4096
NC = 2048


def spread(value, axis, source):
    kept = jnp.where(lax.axis_index(axis) == source, value, 0).astype(value.dtype)
    return lax.psum(kept, axis)


def local(root_inverse, child_coupling, child_inverse, pattern):
    highest = lax.Precision.HIGHEST
    rows_axis = lax.axis_size("row")
    cols_axis = lax.axis_size("col")
    my_row = lax.axis_index("row")
    root_blocks, width, col_blocks, _ = root_inverse.shape
    child_count = child_coupling.shape[0]
    child_columns = child_coupling.shape[3]
    local_rows = root_blocks * width
    block_ids = jnp.arange(root_blocks, dtype=jnp.int32) * rows_axis + my_row
    matches = (jnp.arange(NR // B, dtype=jnp.int32)[None, :] == block_ids[:, None]).astype(
        jnp.float32
    )
    keep = jnp.einsum("jn,an->ja", pattern.astype(jnp.float32), matches)
    coupled = child_coupling * keep[:, :, None, None, None]
    root_panel, child_panel = (
        lax.all_gather(root_inverse, "row", axis=1, tiled=True),
        lax.all_gather(child_inverse, "row", axis=2, tiled=True),
    )
    columns = root_panel.reshape(NR, col_blocks * width)
    groups = rows_axis // cols_axis
    chosen = lax.dynamic_index_in_dim(
        columns.reshape(NR, root_blocks, groups, width), my_row // cols_axis, 2, False
    )
    mirrored = spread(chosen.reshape(NR, local_rows), "col", my_row % cols_axis)
    sigma_local = jnp.einsum("km,kn->mn", mirrored, columns, precision=highest)
    sigma_root = sigma_local.reshape(root_blocks, width, col_blocks, width)
    sigma_rows, coupling_rows = (
        lax.all_gather(sigma_root, "col", axis=3, tiled=True),
        lax.all_gather(coupled, "col", axis=4, tiled=True),
    )
    coupling_panel = coupling_rows.reshape(child_count, local_rows, NC)
    inverse_columns = child_panel.reshape(child_count, NC, child_columns * width)
    update = jnp.einsum("jmk,jkn->jmn", coupling_panel, inverse_columns, precision=highest)
    sigma_split = sigma_rows.reshape(local_rows, root_blocks, rows_axis * width)
    update_split = update.reshape(child_count, root_blocks, width, child_columns * width)
    product = jnp.einsum(
        "mak,jakn->jmn",
        sigma_split,
        lax.all_gather(update_split, "row", axis=2, tiled=True),
        precision=highest,
    )
    coupling_sigma = -(
        product.reshape(child_count, root_blocks, width, child_columns * width)
        * keep[:, :, None, None]
    )
    local_inverse = child_inverse.reshape(child_count, -1, child_columns, width)
    first_part = jnp.einsum("jkcr,jkcs->jcrs", local_inverse, local_inverse, precision=highest)
    update_blocks = update.reshape(child_count, local_rows, child_columns, width)
    sigma_blocks = coupling_sigma.reshape(child_count, local_rows, child_columns, width)
    second_part = jnp.einsum("jkcr,jkcs->jcrs", update_blocks, sigma_blocks, precision=highest)
    summed = lax.psum(first_part - second_part, "row")
    sigma_child = summed.transpose(0, 2, 1, 3)
    return (
        sigma_root,
        coupling_sigma.reshape(child_count, root_blocks, width, child_columns, width),
        sigma_child,
    )


def solution(mesh):
    in_specs = (
        P(None, "row", None, "col"),
        P(None, None, "row", None, "col"),
        P(None, None, "row", None, "col"),
        P(),
    )
    out_specs = (
        P(None, "row", None, "col"),
        P(None, None, "row", None, "col"),
        P(None, None, None, "col"),
    )
    return jax.shard_map(local, mesh=mesh, in_specs=in_specs, out_specs=out_specs, check_vma=False)
```

profile of v0, /device:TPU:0, one launch (start us, length us, event | category | flops | bytes accessed | tf_op | source)
XLA Modules:
  0.0 490.8 jit_solution(11845554919135694700)
XLA Ops:
  7.2 0.0 all-gather.6.cloned.1.call-start
  7.2 0.7 all-gather.6.cloned.1.call-update
  7.9 0.0 all-reduce.3.cloned.1.call-start
  8.0 75.6 %all-gather.6.cloned.1.call-done = f32[2,2048,4,128]{3,2,1,0:T(4,128)} async-done(((f32[2,128,4,128]{3,2,1,0:T(4,128)}), f32[2,2048,4,128]{3,2,1,0:T(4,128)}) %all-gather.6.cloned.1.call-update) | async-done | bytes 8388624 | tf_op jit(solution)/shard_map/all_gather | solution.py:32
  83.6 7.3 %broadcast_select_fusion = f32[4096,2,1,128]{3,2,1,0:T(1,128)} fusion(pred[]{:T(512)S(6)} %eq.18, f32[4096,2,2,128]{3,2,1,0:T(2,128)} %bitcast.53, s32[]{:T(128)S(6)} %select_n.29), kind=kLoop, calls=%fused_computation.1 | loop fusion | flops 1048576 | bytes 8388613 | tf_op jit(solution)/shard_map/jit(_where)/select_n | solution.py:12
  90.8 10.2 %copy.19 = f32[4096,2,1,128]{0,3,1,2:T(8,128)} copy(f32[4096,2,1,128]{3,2,1,0:T(1,128)} %broadcast_select_fusion) | data formatting | bytes 8388608 | tf_op jit(solution)/shard_map/jit(_where)/select_n | solution.py:12
  101.0 0.0 copy-start.3
  101.0 0.0 copy-start.2
  101.0 0.0 all-reduce.3.cloned.1.call-update
  101.0 0.0 all-gather.8.cloned.1.call-start
  101.1 0.6 copy-done.3
  101.7 0.2 convolution_bitcast_fusion
  101.9 0.1 copy.21
  102.0 0.1 copy-done.2
  102.1 1.0 broadcast_multiply_fusion
  103.1 0.0 all-gather.8.cloned.1.call-update
  103.1 0.0 all-gather.10.cloned.1.call-start
  103.2 0.5 all-gather.10.cloned.1.call-update
  103.7 0.0 all-gather.14.cloned.1.call-start
  103.7 7.6 %copy.44 = f32[512,8,4,128]{3,1,2,0:T(8,128)} copy(f32[512,8,4,128]{3,2,1,0:T(4,128)} %bitcast.54) | data formatting | bytes 16777216
  111.3 9.0 %copy.20 = f32[4096,512]{0,1:T(8,128)} copy(f32[4096,512]{1,0:T(8,128)} %bitcast.52) | data formatting | bytes 16777216 | tf_op jit(solution)/shard_map/reshape | solution.py:35
  120.3 53.0 %all-reduce.3.cloned.1.call-done = f32[2,128,4096]{2,1,0:T(8,128)} async-done(((f32[2,128,4096]{2,1,0:T(8,128)}), f32[2,128,4096]{2,1,0:T(8,128)}) %all-reduce.3.cloned.1.call-update) | async-done | bytes 4194320 | tf_op jit(solution)/shard_map/psum | solution.py:13
  173.3 11.0 %fusion = f32[2,128,4,128]{3,1,2,0:T(8,128)} fusion(f32[4,128,4096,1]{2,1,0,3:T(8,128)} %bitcast.51, f32[2,128,4096]{2,1,0:T(8,128)} %all-reduce.3.cloned.1.call-done), kind=kOutput, calls=%fused_computation.2 | convolution fusion | flops 6442450944 | bytes 13107200 | tf_op jit(solution)/shard_map/km,kn->mn/dot_general | solution.py:41
  184.3 0.0 all-gather.14.cloned.1.call-update
  184.3 0.0 all-gather.12.cloned.1.call-start
  184.4 27.3 %all-gather.8.cloned.1.call-done = f32[2,2,128,2,1024]{4,3,2,1,0:T(2,128)} async-done(((f32[2,2,128,2,128]{4,3,2,1,0:T(2,128)}), f32[2,2,128,2,1024]{4,3,2,1,0:T(2,128)}) %all-gather.8.cloned.1.call-update) | async-done | bytes 4194320 | tf_op jit(solution)/shard_map/all_gather | solution.py:45
  211.7 6.6 %reshape.53 = f32[2,256,2048]{2,1,0:T(8,128)} reshape(f32[2,2,128,2,1024]{4,3,2,1,0:T(2,128)} %all-gather.8.cloned.1.call-done) | data formatting | bytes 8388608 | tf_op jit(solution)/shard_map/reshape | solution.py:47
  218.3 48.1 %all-gather.10.cloned.1.call-done = f32[2,1,2048,2,128]{4,3,2,1,0:T(2,128)} async-done(((f32[2,1,128,2,128]{4,3,2,1,0:T(2,128)}), f32[2,1,2048,2,128]{4,3,2,1,0:T(2,128)}) %all-gather.10.cloned.1.call-update) | async-done | bytes 4194320 | tf_op jit(solution)/shard_map/all_gather | solution.py:33
  266.4 6.4 %reshape.54 = f32[2,2048,256]{2,1,0:T(8,128)} reshape(f32[2,1,2048,2,128]{4,3,2,1,0:T(2,128)} %all-gather.10.cloned.1.call-done) | data formatting | bytes 8388608 | tf_op jit(solution)/shard_map/reshape | solution.py:48
  272.9 8.1 %fusion.14 = f32[2,256,256]{2,1,0:T(8,128)S(1)} fusion(f32[2,256,2048]{2,1,0:T(8,128)} %reshape.53, f32[2,2048,256]{2,1,0:T(8,128)} %reshape.54), kind=kOutput, calls=%fused_computation.23 | convolution fusion | flops 3221225472 | bytes 8912896 | tf_op jit(solution)/shard_map/jmk,jkn->jmn/dot_general | solution.py:49
  280.9 1.0 copy.22
  281.9 0.0 all-gather.12.cloned.1.call-update
  282.0 0.2 all-reduce.5.cloned.1.call-start
  282.2 0.1 broadcast_bitcast_fusion
  282.3 0.2 copy.37
  282.5 21.7 %all-gather.14.cloned.1.call-done = f32[2,128,4,1024]{3,1,2,0:T(8,128)} async-done(((f32[2,128,4,128]{3,1,2,0:T(8,128)}), f32[2,128,4,1024]{3,1,2,0:T(8,128)}) %all-gather.14.cloned.1.call-update) | async-done | bytes 4194320 | tf_op jit(solution)/shard_map/all_gather | solution.py:44
  304.2 7.3 %copy.23 = f32[2,128,4,1024]{1,0,3,2:T(2,128)} copy(f32[2,128,4,1024]{3,1,2,0:T(8,128)} %all-gather.14.cloned.1.call-done) | data formatting | bytes 8388608 | tf_op jit(solution)/shard_map/all_gather | solution.py:44
  311.5 6.4 %reshape.56 = f32[256,2,2048]{0,2,1:T(8,128)} reshape(f32[2,128,4,1024]{1,0,3,2:T(2,128)} %copy.23) | data formatting | bytes 8388608 | tf_op jit(solution)/shard_map/reshape | solution.py:50
  317.9 0.0 copy-start.1
  317.9 0.0 copy-start
  317.9 68.3 %all-gather.12.cloned.1.call-done = f32[2,2,2048,256]{2,3,1,0:T(8,128)} async-done(((f32[2,2,128,256]{2,3,1,0:T(8,128)}), f32[2,2,2048,256]{2,3,1,0:T(8,128)}) %all-gather.12.cloned.1.call-update) | async-done | bytes 8388624 | tf_op jit(solution)/shard_map/all_gather | solution.py:55
  386.2 9.8 %fusion.2 = f32[2,256,256,1]{2,1,3,0:T(8,128)S(1)} fusion(f32[2,2,2048,256]{2,3,1,0:T(8,128)} %all-gather.12.cloned.1.call-done, f32[256,2,2048]{0,2,1:T(8,128)} %reshape.56), kind=kOutput, calls=%fused_computation.4 | convolution fusion | flops 6442450944 | bytes 13107200 | tf_op jit(solution)/shard_map/mak,jakn->jmn/dot_general | solution.py:52
  396.0 0.2 copy.29
  396.2 0.8 fusion.5
  397.0 0.0 copy-done.1
  397.0 1.3 fusion.4
  398.3 0.0 all-reduce.5.cloned.1.call-update
  398.3 0.0 copy-done
  398.3 1.1 copy.31
  399.5 0.3 reshape.57
  399.7 0.4 copy.25
  400.2 1.1 multiply_negate_fusion
  401.2 80.9 %all-reduce.5.cloned.1.call-done = f32[2,128,2,128]{3,1,2,0:T(8,128)} async-done(((f32[2,128,2,128]{3,1,2,0:T(8,128)}), f32[2,128,2,128]{3,1,2,0:T(8,128)}) %all-reduce.5.cloned.1.call-update) | async-done | bytes 262160 | tf_op jit(solution)/shard_map/psum | solution.py:67
  482.1 1.9 copy.32
  (2 shorter events, 0.0 us)
Async XLA Ops:
  7.2 76.4 %all-gather.6.cloned.1.call-start = ((), (), s32[]{:S(2)}) async-start(), calls=%async_computation | async-start | bytes 8912896 | tf_op jit(solution)/shard_map/all_gather | solution.py:32
  7.9 165.4 %all-reduce.3.cloned.1.call-start = ((), (), s32[]{:S(2)}) async-start(), calls=%async_computation.1 | async-start | bytes 8388608 | tf_op jit(solution)/shard_map/psum | solution.py:13
  101.0 0.7 copy-start.3
  101.0 1.1 copy-start.2
  101.0 110.6 %all-gather.8.cloned.1.call-start = ((), (), s32[]{:S(2)}) async-start(), calls=%async_computation.2 | async-start | bytes 4718592 | tf_op jit(solution)/shard_map/all_gather | solution.py:45
  103.1 163.3 %all-gather.10.cloned.1.call-start = ((), (), s32[]{:S(2)}) async-start(), calls=%async_computation.3 | async-start | bytes 4456448 | tf_op jit(solution)/shard_map/all_gather | solution.py:33
  103.7 200.5 %all-gather.14.cloned.1.call-start = ((), (), s32[]{:S(2)}) async-start(), calls=%async_computation.5 | async-start | bytes 4718592 | tf_op jit(solution)/shard_map/all_gather | solution.py:44
  184.3 201.9 %all-gather.12.cloned.1.call-start = ((), (), s32[]{:S(2)}) async-start(), calls=%async_computation.4 | async-start | bytes 8912896 | tf_op jit(solution)/shard_map/all_gather | solution.py:55
  282.0 200.1 %all-reduce.5.cloned.1.call-start = ((), (), s32[]{:S(2)}) async-start(), calls=%async_computation.6 | async-start | bytes 524288 | tf_op jit(solution)/shard_map/psum | solution.py:67
  317.9 79.1 %copy-start.1 = (f32[2,1,128,2,128]{4,3,2,1,0:T(2,128)S(1)}, f32[2,1,128,2,128]{4,3,2,1,0:T(2,128)}, u32[]{:S(2)}) copy-start(f32[2,1,128,2,128]{4,3,2,1,0:T(2,128)} %param.6) | copy-start | bytes 786436
  317.9 80.4 %copy-start = (f32[2,128,4,128]{3,1,2,0:T(8,128)S(1)}, f32[2,128,4,128]{3,1,2,0:T(8,128)}, u32[]{:S(2)}) copy-start(f32[2,128,4,128]{3,1,2,0:T(8,128)} %fusion) | copy-start | bytes 1572868
Sparse Core Ops, SparseCore 0:
  10.2 73.3 all-gather.5
  101.1 72.0 all-reduce.2
  175.5 36.0 all-gather.7
  213.7 52.6 all-gather.9
  268.5 35.6 all-gather.13
  306.7 79.4 all-gather.11
  398.4 83.6 all-reduce.4
where the time goes:
time: 492 us; the launch traced here: 491 us
  waiting for transfers between devices  376 us (76%)
  local copies, waits for them, and re-layouts  59.4 us (12%)
  matrix products  31.1 us (6%)
  between operations  14.2 us (3%)
  other arithmetic  9.37 us (2%)
    psum x1, waiting for transfers between devices, local(): summed = lax.psum(first_part - second_part, 'row')  80.9 us
    all_gather x1, waiting for transfers between devices, local(): lax.all_gather(root_inverse, 'row', axis=1, tiled=True)  75.6 us
    all_gather x1, waiting for transfers between devices, local(): lax.all_gather(update_split, 'row', axis=2, tiled=True)  68.3 us
    psum x1, waiting for transfers between devices, spread(): return lax.psum(kept, axis)  53 us
    all_gather x1, waiting for transfers between devices, local(): lax.all_gather(child_inverse, 'row', axis=2, tiled=True)  48.1 us
    all_gather x1, waiting for transfers between devices, local(): lax.all_gather(coupled, 'col', axis=4, tiled=True)  27.3 us
    all_gather x1, waiting for transfers between devices, local(): lax.all_gather(sigma_root, 'col', axis=3, tiled=True)  21.7 us
    unnamed x13, local copies, waits for them, and re-layouts  11.4 us
  transfers between devices with their start and end apart: 7, of which 7 were waited for; matrix products, arithmetic and copies ran while one was open for 14% of the time, Pallas kernels for 0%

commit v1 on v0

--- a/solution.py
+++ b/solution.py
@@ -30,7 +30,9 @@
     coupled = child_coupling * keep[:, :, None, None, None]
     root_panel, child_panel = (
         lax.all_gather(root_inverse, "row", axis=1, tiled=True),
-        lax.all_gather(child_inverse, "row", axis=2, tiled=True),
+        jnp.concatenate(
+            lax.all_to_all(jnp.stack([child_inverse] * lax.axis_size("row")), "row", 0, 0), axis=2
+        ),
     )
     columns = root_panel.reshape(NR, col_blocks * width)
     groups = rows_axis // cols_axis

time: 492 us -> 449 us (0.913)
  waiting for transfers between devices: 376 us -> 273 us
  blocking collectives: 0 us -> 55.8 us
    all_to_all x0 -> x1, blocking collectives: none -> 55.8 us  [local(): lax.all_to_all(jnp.stack([child_inverse] * lax.axis_size('row')), 'row',...]
    all_gather x1 -> x0, waiting for transfers between devices: 48.1 us -> none  [local(): lax.all_gather(child_inverse, 'row', axis=2, tiled=True)]
    all_gather x1, waiting for transfers between devices: 27.3 us -> 0.01 us  [local(): lax.all_gather(coupled, 'col', axis=4, tiled=True)]
    all_gather x1, waiting for transfers between devices: 21.7 us -> 0.02 us  [local(): lax.all_gather(sigma_root, 'col', axis=3, tiled=True)]
    another operation x0 -> x2, local copies, waits for them, and re-layouts: none -> 8.33 us  [the longest x1 6.45 us: local(): child_panel.reshape(child_count, NC, child_columns * width)]
    all_gather x1, waiting for transfers between devices: 68.3 us -> 62.1 us  [local(): lax.all_gather(update_split, 'row', axis=2, tiled=True)]
  transfers between devices with their start and end apart: 7 -> 6, of which waited for: 7 -> 4; matrix products, arithmetic and copies ran while one was open for 14% -> 16% of each run, Pallas kernels for 0% -> 0%
where the time goes in v1:
time: 449 us; the launch traced here: 448 us
  waiting for transfers between devices  273 us (61%)
  local copies, waits for them, and re-layouts  63.8 us (14%)
  blocking collectives  55.8 us (12%)
  matrix products  31.2 us (7%)
  between operations  14.2 us (3%)
  other arithmetic  9.37 us (2%)
    psum x1, waiting for transfers between devices, local(): summed = lax.psum(first_part - second_part, 'row')  80.9 us
    all_gather x1, waiting for transfers between devices, local(): lax.all_gather(root_inverse, 'row', axis=1, tiled=True)  75.6 us
    all_gather x1, waiting for transfers between devices, local(): lax.all_gather(update_split, 'row', axis=2, tiled=True)  62.1 us
    all_to_all x1, blocking collectives, local(): lax.all_to_all(jnp.stack([child_inverse] * lax.axis_size('row')), 'row',...  55.8 us
    psum x1, waiting for transfers between devices, spread(): return lax.psum(kept, axis)  53.4 us
    unnamed x13, local copies, waits for them, and re-layouts  11.4 us
    dot_general x1, matrix products, local(): sigma_local = jnp.einsum('km,kn->mn', mirrored, columns, precision=highest)  11.1 us
    select_n x1, local copies, waits for them, and re-layouts, spread(): jnp.where(lax.axis_index(axis) == source, value, 0).astype(value.dtype)  10.2 us
  transfers between devices with their start and end apart: 6, of which 4 were waited for; matrix products, arithmetic and copies ran while one was open for 16% of the time, Pallas kernels for 0%

profile of v1, /device:TPU:0, one launch (start us, length us, event | category | flops | bytes accessed | tf_op | source)
XLA Modules:
  0.0 447.6 jit_solution(11983066105440679032)
XLA Ops:
  7.2 0.0 all-gather.5.cloned.1.call-start
  7.2 0.7 all-gather.5.cloned.1.call-update
  7.9 0.0 all-reduce.3.cloned.1.call-start
  8.0 75.6 %all-gather.5.cloned.1.call-done = f32[2,2048,4,128]{3,2,1,0:T(4,128)} async-done(((f32[2,128,4,128]{3,2,1,0:T(4,128)}), f32[2,2048,4,128]{3,2,1,0:T(4,128)}) %all-gather.5.cloned.1.call-update) | async-done | bytes 8388624 | tf_op jit(solution)/shard_map/all_gather | solution.py:32
  83.6 7.2 %broadcast_select_fusion = f32[4096,2,1,128]{3,2,1,0:T(1,128)} fusion(pred[]{:T(512)S(6)} %eq.18, f32[4096,2,2,128]{3,2,1,0:T(2,128)} %bitcast.56, s32[]{:T(128)S(6)} %select_n.29), kind=kLoop, calls=%fused_computation.1 | loop fusion | flops 1048576 | bytes 8388613 | tf_op jit(solution)/shard_map/jit(_where)/select_n | solution.py:12
  90.8 10.2 %copy.33 = f32[4096,2,1,128]{0,3,1,2:T(8,128)} copy(f32[4096,2,1,128]{3,2,1,0:T(1,128)} %broadcast_select_fusion) | data formatting | bytes 8388608 | tf_op jit(solution)/shard_map/jit(_where)/select_n | solution.py:12
  101.0 0.0 copy-start.3
  101.0 0.0 copy-start.2
  101.0 0.0 all-reduce.3.cloned.1.call-update
  101.0 0.0 all-gather.7.cloned.1.call-start
  101.1 0.6 copy-done.3
  101.7 0.2 convolution_bitcast_fusion
  101.9 0.1 copy.35
  102.0 0.1 copy-done.2
  102.1 1.0 broadcast_multiply_fusion
  103.1 0.0 all-gather.7.cloned.1.call-update
  103.1 0.0 all-gather.11.cloned.1.call-start
  103.2 7.6 %copy.59 = f32[512,8,4,128]{3,1,2,0:T(8,128)} copy(f32[512,8,4,128]{3,2,1,0:T(4,128)} %bitcast.57) | data formatting | bytes 16777216
  110.8 9.1 %copy.34 = f32[4096,512]{0,1:T(8,128)} copy(f32[4096,512]{1,0:T(8,128)} %bitcast.55) | data formatting | bytes 16777216 | tf_op jit(solution)/shard_map/reshape | solution.py:37
  119.9 53.4 %all-reduce.3.cloned.1.call-done = f32[2,128,4096]{2,1,0:T(8,128)} async-done(((f32[2,128,4096]{2,1,0:T(8,128)}), f32[2,128,4096]{2,1,0:T(8,128)}) %all-reduce.3.cloned.1.call-update) | async-done | bytes 4194320 | tf_op jit(solution)/shard_map/psum | solution.py:13
  173.3 0.0 copy-start.1
  173.3 11.1 %fusion = f32[2,128,4,128]{3,1,2,0:T(8,128)} fusion(f32[4,128,4096,1]{2,1,0,3:T(8,128)} %bitcast.54, f32[2,128,4096]{2,1,0:T(8,128)} %all-reduce.3.cloned.1.call-done), kind=kOutput, calls=%fused_computation.2 | convolution fusion | flops 6442450944 | bytes 13107200 | tf_op jit(solution)/shard_map/km,kn->mn/dot_general | solution.py:43
  184.3 0.0 all-gather.11.cloned.1.call-update
  184.4 0.0 all-gather.9.cloned.1.call-start
  184.4 0.0 copy-done.1
  184.4 1.9 stack.2
  186.3 55.8 %all_to_all.5 = f32[16,2,1,128,2,128]{5,4,3,1,2,0:T(2,128)S(1)} all-to-all(f32[16,2,1,128,2,128]{5,4,3,1,2,0:T(2,128)S(1)} %stack.2), channel_id=1, replica_groups=mesh['row'=16,'col'=8] {'row'}, dimensions={0} | all-to-all | bytes 8388608 | tf_op jit(solution)/shard_map/all_to_all | solution.py:34
  242.1 2.3 copy.36
  244.4 6.5 %reshape_reshape.7 = f32[2,2048,256]{2,1,0:T(8,128)} reshape(f32[2,1,16,128,2,128]{5,4,3,2,0,1:T(2,128)} %copy.36) | data formatting | bytes 8388608 | tf_op jit(solution)/shard_map/reshape;reshape | solution.py:50
  250.8 0.0 all-gather.7.cloned.1.call-done
  250.8 6.6 %reshape.54 = f32[2,256,2048]{2,1,0:T(8,128)} reshape(f32[2,2,128,2,1024]{4,3,2,1,0:T(2,128)} %all-gather.7.cloned.1.call-done) | data formatting | bytes 8388608 | tf_op jit(solution)/shard_map/reshape | solution.py:49
  257.5 8.1 %fusion.14 = f32[2,256,256]{2,1,0:T(8,128)S(1)} fusion(f32[2,256,2048]{2,1,0:T(8,128)} %reshape.54, f32[2,2048,256]{2,1,0:T(8,128)} %reshape_reshape.7), kind=kOutput, calls=%fused_computation.23 | convolution fusion | flops 3221225472 | bytes 8912896 | tf_op jit(solution)/shard_map/jmk,jkn->jmn/dot_general | solution.py:51
  265.5 1.0 copy.37
  266.5 0.0 all-gather.9.cloned.1.call-update
  266.6 0.3 all-reduce.5.cloned.1.call-start
  266.8 0.1 broadcast_bitcast_fusion
  266.9 0.2 copy.52
  267.1 0.0 all-gather.11.cloned.1.call-done
  267.1 7.3 %copy.38 = f32[2,128,4,1024]{1,0,3,2:T(2,128)} copy(f32[2,128,4,1024]{3,1,2,0:T(8,128)} %all-gather.11.cloned.1.call-done) | data formatting | bytes 8388608 | tf_op jit(solution)/shard_map/all_gather | solution.py:46
  274.4 6.5 %reshape.57 = f32[256,2,2048]{0,2,1:T(8,128)} reshape(f32[2,128,4,1024]{1,0,3,2:T(2,128)} %copy.38) | data formatting | bytes 8388608 | tf_op jit(solution)/shard_map/reshape | solution.py:52
  280.9 0.0 copy-start
  280.9 62.1 %all-gather.9.cloned.1.call-done = f32[2,2,2048,256]{2,3,1,0:T(8,128)} async-done(((f32[2,2,128,256]{2,3,1,0:T(8,128)}), f32[2,2,2048,256]{2,3,1,0:T(8,128)}) %all-gather.9.cloned.1.call-update) | async-done | bytes 8388624 | tf_op jit(solution)/shard_map/all_gather | solution.py:57
  343.0 9.8 %fusion.2 = f32[2,256,256,1]{2,1,3,0:T(8,128)S(1)} fusion(f32[2,2,2048,256]{2,3,1,0:T(8,128)} %all-gather.9.cloned.1.call-done, f32[256,2,2048]{0,2,1:T(8,128)} %reshape.57), kind=kOutput, calls=%fused_computation.4 | convolution fusion | flops 6442450944 | bytes 13107200 | tf_op jit(solution)/shard_map/mak,jakn->jmn/dot_general | solution.py:54
  352.8 0.2 copy.44
  353.0 0.8 fusion.5
  353.8 1.3 fusion.4
  355.1 0.0 all-reduce.5.cloned.1.call-update
  355.1 0.0 copy-done
  355.1 1.1 copy.46
  356.3 0.3 reshape.58
  356.5 0.4 copy.40
  357.0 1.1 multiply_negate_fusion
  358.0 80.9 %all-reduce.5.cloned.1.call-done = f32[2,128,2,128]{3,1,2,0:T(8,128)} async-done(((f32[2,128,2,128]{3,1,2,0:T(8,128)}), f32[2,128,2,128]{3,1,2,0:T(8,128)}) %all-reduce.5.cloned.1.call-update) | async-done | bytes 262160 | tf_op jit(solution)/shard_map/psum | solution.py:69
  438.9 1.9 copy.47
  (2 shorter events, 0.0 us)
Async XLA Ops:
  7.2 76.4 %all-gather.5.cloned.1.call-start = ((), (), s32[]{:S(2)}) async-start(), calls=%async_computation.1 | async-start | bytes 8912896 | tf_op jit(solution)/shard_map/all_gather | solution.py:32
  7.9 165.4 %all-reduce.3.cloned.1.call-start = ((), (), s32[]{:S(2)}) async-start(), calls=%async_computation.2 | async-start | bytes 8388608 | tf_op jit(solution)/shard_map/psum | solution.py:13
  101.0 0.7 copy-start.3
  101.0 1.1 copy-start.2
  101.0 149.8 %all-gather.7.cloned.1.call-start = ((), (), s32[]{:S(2)}) async-start(), calls=%async_computation.3 | async-start | bytes 4718592 | tf_op jit(solution)/shard_map/all_gather | solution.py:47
  103.1 164.0 %all-gather.11.cloned.1.call-start = ((), (), s32[]{:S(2)}) async-start(), calls=%async_computation.5 | async-start | bytes 4718592 | tf_op jit(solution)/shard_map/all_gather | solution.py:46
  173.3 11.1 %copy-start.1 = (f32[2,1,128,2,128]{4,3,2,1,0:T(2,128)S(1)}, f32[2,1,128,2,128]{4,3,2,1,0:T(2,128)}, u32[]{:S(2)}) copy-start(f32[2,1,128,2,128]{4,3,2,1,0:T(2,128)} %param.6) | copy-start | bytes 786436
  184.4 158.7 %all-gather.9.cloned.1.call-start = ((), (), s32[]{:S(2)}) async-start(), calls=%async_computation.4 | async-start | bytes 8912896 | tf_op jit(solution)/shard_map/all_gather | solution.py:57
  266.6 172.4 %all-reduce.5.cloned.1.call-start = ((), (), s32[]{:S(2)}) async-start(), calls=%async_computation.6 | async-start | bytes 524288 | tf_op jit(solution)/shard_map/psum | solution.py:69
  280.9 74.2 %copy-start = (f32[2,128,4,128]{3,1,2,0:T(8,128)S(1)}, f32[2,128,4,128]{3,1,2,0:T(8,128)}, u32[]{:S(2)}) copy-start(f32[2,128,4,128]{3,1,2,0:T(8,128)} %fusion) | copy-start | bytes 1572868
Sparse Core Ops, SparseCore 0:
  10.2 73.3 all-gather.4
  101.1 72.0 all-reduce.2
  175.5 36.0 all-gather.6
  213.8 37.0 all-gather.10
  266.7 76.2 all-gather.8
  355.2 83.6 all-reduce.4
